TPU v7x, 32 devices: a whole 2x2x4 slice. The times are simulated.
32 devices in a mesh: ctx: 8 (over y, x, core), head: 4 (over z).
Axes of the slice: x: 2, y: 2, z: 4, core: 2. Of those that a mesh axis runs over, the one named last changes fastest.
Arguments:
- channels: bfloat16 [6144, 4096], P(('ctx', 'head')), may hold values from -6 to 6
- input_state_factors: bfloat16 [6144, 128], P(('ctx', 'head')), may hold values from -6 to 6
- c_coeffs: bfloat16 [6144, 128], P(('ctx', 'head')), may hold values from -6 to 6
- step_size_logits: bfloat16 [6144, 64], P(('ctx', 'head'))
- a_log: float32 [64], P('head')
- skip_gain: float32 [64], P('head'), may hold values from 0.5 to 1.5
- mix_gain: float32 [64, 3], P('head'), may hold values from -0.6 to 0.6
- offsets: int32 [48, 3], P('ctx'), may hold values from 1 to 3, as said below
- cotangent: bfloat16 [6144, 4096], P('ctx', 'head'), may hold values from -6 to 6
Outputs:
- mixed: bfloat16 [6144, 4096], P('ctx', 'head')
- grad_channels: bfloat16 [6144, 4096], P(('ctx', 'head'))
- grad_b: float32 [6144, 128], P(('ctx', 'head'))
- grad_c: float32 [6144, 128], P(('ctx', 'head'))
Inputs may be any that keep to these rules, and one draw needn't show every extreme that they name: Each block's 3 offsets are distinct; block b's neighbour in slot k is block b - offsets[b, k], and there is none where that index is negative.
All inputs are finite; a program needn't handle non-finite values.
Results may differ from a plain program's by a relative error of at most 0.0052.
Values may be sent and summed in bfloat16 or wider, within the bound.
A program may use at most 128 MiB of HBM per device.

v0:
```python
import math

import jax
import jax.numpy as jnp
from jax import lax
from jax.experimental import pallas as pl
from jax.experimental.pallas import tpu as pltpu
from jax.sharding import PartitionSpec as P

P_SIZE = 64
N = 128
Q = 128
F32 = jnp.float32
BF16 = jnp.bfloat16
VMEM_BYTES = 56 * 1024 * 1024


def dot(left, right, dims, precision=None):
    return lax.dot_general(
        left, right, (dims, ((), ())), preferred_element_type=F32, precision=precision
    )


def iota(shape, dim):
    return lax.broadcasted_iota(jnp.int32, shape, dim)


def halves(value):
    high = value.astype(BF16)
    return high, (value - high.astype(F32)).astype(BF16)


def head_of_column(heads):
    shape = (heads, heads * P_SIZE)
    first = iota(shape, 0) * P_SIZE
    column = iota(shape, 1)
    return ((column >= first) & (column < first + P_SIZE)).astype(F32).astype(BF16)


def over_columns(value, spread):
    high, low = halves(value)
    return dot(high, spread, ((1,), (0,))) + dot(low, spread, ((1,), (0,)))


def over_rows(column, spread):
    high, low = halves(jnp.broadcast_to(column, (column.shape[0], N)))
    return dot(spread, high, ((0,), (0,))) + dot(spread, low, ((0,), (0,)))


def two_heads(value):
    lower = iota(value.shape, 1) < P_SIZE
    zero = jnp.zeros_like(value)
    return jnp.concatenate([jnp.where(lower, value, zero), jnp.where(lower, zero, value)], axis=0)


def remote(source, target, send, recv, axis, place):
    return pltpu.make_async_remote_copy(
        src_ref=source,
        dst_ref=target,
        send_sem=send,
        recv_sem=recv,
        device_id={axis: place},
        device_id_type=pl.DeviceIdType.MESH,
    )


def mixer_kernel(
    groups, ctx, spans, reach, in_scale,
    chan_in, b_in, c_in, dt_in, a_log, skip, gain, offs, cot_in,
    mixed, gx, gb, gc,
    cot, off, b_all, c_all, dt_all, chan, g, cum_all, cumt_all, full, pay_g, ends_g, pay_s, ends_s,
    pieces, dx, starts, y_intra, db, dc, grads, parts, out, carry, running,
    z_send, z_recv, c_send, c_recv, n_send, n_recv, local,
):
    heads = a_log.shape[1]
    width = heads * P_SIZE
    tok_dev = chan_in.shape[0]
    slots = gain.shape[0]
    me = lax.axis_index("head")
    place = lax.axis_index("ctx")
    spread = head_of_column(heads)

    def token_rows(index):
        return pl.ds(pl.multiple_of(index * tok_dev, 64), tok_dev)

    def wide(index):
        return pl.ds(pl.multiple_of(index * width, 128), width)

    def span_rows(span):
        return pl.ds(pl.multiple_of(span * Q, Q), Q)

    barrier = pltpu.get_barrier_semaphore()
    for shift in range(1, groups):
        pl.semaphore_signal(
            barrier, inc=1, device_id={"head": lax.rem(me + shift, groups)},
            device_id_type=pl.DeviceIdType.MESH,
        )
    for shift in range(1, ctx):
        pl.semaphore_signal(
            barrier, inc=1, device_id={"ctx": lax.rem(place + shift, ctx)},
            device_id_type=pl.DeviceIdType.MESH,
        )
    own = [
        pltpu.make_async_copy(b_in, b_all.at[token_rows(me), :], local.at[0]),
        pltpu.make_async_copy(c_in, c_all.at[token_rows(me), :], local.at[1]),
        pltpu.make_async_copy(dt_in, dt_all.at[token_rows(me), :], local.at[2]),
        pltpu.make_async_copy(cot_in, cot.at[pl.ds(0, spans * Q), :], local.at[3]),
        pltpu.make_async_copy(offs, off.at[pl.ds(0, spans)], local.at[4]),
        pltpu.make_async_copy(chan_in.at[:, wide(me)], chan.at[token_rows(me), :], local.at[5]),
    ]
    for copy in own:
        copy.start()
    pl.semaphore_wait(barrier, groups - 1 + ctx - 1)

    small, large = [], []
    for shift in range(1, groups):
        target = lax.rem(me + shift, groups)
        for kind, (source, home) in enumerate(((b_in, b_all), (c_in, c_all), (dt_in, dt_all))):
            small.append(
                remote(
                    source, home.at[token_rows(me), :], z_send.at[kind, shift],
                    z_recv.at[kind, shift], "head", target,
                )
            )
        large.append(
            remote(
                chan_in.at[:, wide(target)], chan.at[token_rows(me), :], z_send.at[3, shift],
                z_recv.at[3, shift], "head", target,
            )
        )
    back = lax.rem(place + ctx - 1, ctx)
    onward = lax.rem(place + 1, ctx)
    later = [
        remote(
            offs.at[pl.ds(0, reach)], off.at[pl.ds(spans, reach)], n_send.at[0], n_recv.at[0],
            "ctx", back,
        ),
        remote(
            cot_in.at[pl.ds(0, reach * Q), :], cot.at[pl.ds(spans * Q, reach * Q), :],
            n_send.at[1], n_recv.at[1], "ctx", back,
        ),
    ]
    for copy in small:
        copy.start()

    @pl.when(place > 0)
    def _():
        for copy in later:
            copy.start()

    for copy in large:
        copy.start()

    @pl.when(place == 0)
    def _():
        out[pl.ds(0, reach * Q), :] = jnp.zeros((reach * Q, width), BF16)

    @pl.when(place == ctx - 1)
    def _():
        cot[pl.ds(spans * Q, reach * Q), :] = jnp.zeros((reach * Q, width), BF16)
        off[pl.ds(spans, reach)] = jnp.zeros((reach, 1, N), jnp.int32)

    for copy in own[:5]:
        copy.wait()
    for copy in small:
        copy.wait_recv()

    chosen = (
        iota((dt_all.shape[1], heads), 0) == iota((dt_all.shape[1], heads), 1) + me * heads
    ).astype(F32).astype(BF16)
    tri = (iota((Q, Q), 0) >= iota((Q, Q), 1)).astype(F32)
    rate = -jnp.exp(a_log[...])

    def add_up(span, total):
        rows = span_rows(span)
        steps = dot(dt_all[rows, :], chosen, ((1,), (0,)))
        decay = rate * (jnp.maximum(steps, 0.0) + jnp.log1p(jnp.exp(-jnp.abs(steps))))
        cumt = dot(decay, tri, ((0,), (1,)), lax.Precision.HIGHEST)
        cum_all[rows, :] = dot(tri, decay, ((1,), (0,)), lax.Precision.HIGHEST)
        cumt_all[span] = cumt
        return total + cumt[:, Q - 1 : Q]

    total = lax.fori_loop(0, spans, add_up, jnp.zeros((heads, 1), F32))
    high, low = halves(jnp.broadcast_to(total, (heads, N)))
    lowest = (total - high.astype(F32) - low.astype(F32)).astype(BF16)
    lane = iota((heads, N), 1)
    packed = jnp.where(lane == 0, high, jnp.where(lane == 1, low, lowest))
    pad = pay_g.shape[0] - width
    if pad > heads:
        packed = jnp.concatenate([packed, jnp.zeros((pad - heads, N), BF16)], axis=0)
    pay_g[pl.ds(width, pad), :] = packed
    pay_s[pl.ds(width, pad), :] = packed

    @pl.when(place < ctx - 1)
    def _():
        for copy in later:
            copy.wait_recv()

    def picked(row, far):
        offset = off[row]
        weight = jnp.zeros((1, width), F32)
        for slot in range(slots):
            hit = (offset[:, slot : slot + 1] == far).astype(F32)
            weight = weight + hit * gain[slot : slot + 1, :]
        return weight

    carry[...] = jnp.zeros_like(carry)

    def back_mix(span, earlier):
        rows = span_rows(span)
        grad = cot[rows, :].astype(F32)
        for far in range(1, reach + 1):
            grad = grad + picked(span + far, far) * cot[span_rows(span + far), :].astype(F32)
        grad = grad.astype(BF16)
        g[rows, :] = grad
        scaled = (grad.astype(F32) * over_columns(jnp.exp(cum_all[rows, :]), spread)).astype(BF16)
        flow = dot(scaled, c_all[rows, :], ((0,), (0,)))
        full[span] = flow.astype(BF16)
        carry[...] = carry[...] + over_rows(jnp.exp(earlier), spread) * flow
        return earlier + cumt_all[span][:, Q - 1 : Q]

    lax.fori_loop(0, spans, back_mix, jnp.zeros((heads, 1), F32))
    pay_g[pl.ds(0, width), :] = carry[...].astype(BF16)

    def scan_copies(kind, source, ends, sign):
        return [
            remote(
                source, ends.at[far - 1], c_send.at[kind, far], c_recv.at[kind, far], "ctx",
                lax.rem(place + ctx + sign * far, ctx),
            )
            for far in range(1, ctx)
        ]

    to_earlier = scan_copies(0, pay_g, ends_g, -1)
    to_later = scan_copies(1, pay_s, ends_s, 1)

    def gather_ends(ends, copies, present):
        carry[...] = jnp.zeros_like(carry)
        running[...] = jnp.zeros_like(running)
        for far in range(1, ctx):

            @pl.when(present(far))
            def _(far=far):
                copies[far - 1].wait_recv()
                sums = running[...]
                carry[...] = carry[...] + over_rows(jnp.exp(sums[:, :1]), spread) * ends[
                    far - 1, pl.ds(0, width), :
                ].astype(F32)
                logs = ends[far - 1, pl.ds(width, pad), :].astype(F32)[:heads]
                running[...] = sums + (logs[:, 0:1] + logs[:, 1:2] + logs[:, 2:3])

    for far in range(1, ctx):

        @pl.when(place >= far)
        def _(far=far):
            to_earlier[far - 1].start()

    own[5].wait()
    for copy in large:
        copy.wait_recv()

    def tail_of(rows):
        cum = cum_all[rows, :]
        last = cum[Q - 1 : Q, :]
        return over_columns(jnp.exp(last - cum) * in_scale, spread)

    carry[...] = jnp.zeros_like(carry)

    def add_pieces(span, unused):
        rows = span_rows(span)
        state = carry[...]
        starts[span] = state
        scaled = (chan[rows, :].astype(F32) * tail_of(rows)).astype(BF16)
        added = dot(scaled, b_all[rows, :], ((0,), (0,)))
        carry[...] = over_rows(jnp.exp(cumt_all[span][:, Q - 1 : Q]), spread) * state + added
        return unused

    lax.fori_loop(0, spans, add_pieces, 0)
    pay_s[pl.ds(0, width), :] = carry[...].astype(BF16)
    for far in range(1, ctx):

        @pl.when(place + far < ctx)
        def _(far=far):
            to_later[far - 1].start()

    gather_ends(ends_g, to_earlier, lambda far: place + far < ctx)

    def dx_copy(chunk):
        return remote(
            dx.at[pl.ds(chunk * tok_dev, tok_dev), :], gx.at[:, wide(me)], z_send.at[4, chunk],
            z_recv.at[4, me], "head", chunk,
        )

    def grad_channels(step, unused):
        span = spans - 1 - step
        rows = span_rows(span)
        after = carry[...]
        flow = after.astype(BF16)
        pieces[span] = flow
        b_rows = b_all[rows, :]
        cum = cum_all[rows, :]
        cumt = cumt_all[span]
        from_state = dot(b_rows, flow, ((1,), (1,))) * tail_of(rows)
        scores = dot(b_rows, c_all[rows, :], ((1,), (1,))) * in_scale
        seen = iota((Q, Q), 0) <= iota((Q, Q), 1)
        for pair in range(heads // 2):
            columns = slice(pair * 2 * P_SIZE, (pair + 1) * 2 * P_SIZE)
            weights = []
            for head in (2 * pair, 2 * pair + 1):
                gap = cumt[head : head + 1, :] - cum[:, head : head + 1]
                weights.append((scores * jnp.exp(jnp.where(seen, gap, -1e30))).astype(BF16))
            part = g[rows, columns]
            intra = dot(jnp.concatenate(weights, axis=1), two_heads(part), ((1,), (0,)))
            dx[rows, columns] = (
                intra + from_state[:, columns] + skip[:, columns] * part.astype(F32)
            ).astype(BF16)
        carry[...] = full[span].astype(F32) + over_rows(jnp.exp(cumt[:, Q - 1 : Q]), spread) * after
        for chunk in range(groups):

            @pl.when((span == chunk * tok_dev // Q) & (me != chunk))
            def _(chunk=chunk):
                dx_copy(chunk).start()

        return unused

    lax.fori_loop(0, spans, grad_channels, 0)
    keep = pltpu.make_async_copy(dx.at[token_rows(me), :], gx.at[:, wide(me)], local.at[6])
    keep.start()

    def intra(span, unused):
        rows = span_rows(span)
        b_rows = b_all[rows, :]
        c_rows = c_all[rows, :]
        cum = cum_all[rows, :]
        cumt = cumt_all[span]
        scores = dot(c_rows, b_rows, ((1,), (1,))) * in_scale
        seen = iota((Q, Q), 0) >= iota((Q, Q), 1)
        score_grads = jnp.zeros((Q, Q), F32)
        for pair in range(heads // 2):
            columns = slice(pair * 2 * P_SIZE, (pair + 1) * 2 * P_SIZE)
            chans = chan[rows, columns]
            products = dot(two_heads(g[rows, columns]), chans, ((1,), (1,)))
            weights = []
            for one, head in enumerate((2 * pair, 2 * pair + 1)):
                gap = cum[:, head : head + 1] - cumt[head : head + 1, :]
                decay = jnp.exp(jnp.where(seen, gap, -1e30))
                weights.append((scores * decay).astype(BF16))
                score_grads = score_grads + products[one * Q : (one + 1) * Q, :] * decay
            y_intra[rows, columns] = dot(
                jnp.concatenate(weights, axis=1), two_heads(chans), ((1,), (0,))
            ) + skip[:, columns] * chans.astype(F32)
        score_grads = (score_grads * in_scale).astype(BF16)
        scaled = (chan[rows, :].astype(F32) * tail_of(rows)).astype(BF16)
        dc[rows, :] = dot(score_grads, b_rows, ((1,), (0,)))
        db[rows, :] = dot(score_grads, c_rows, ((0,), (0,))) + dot(
            scaled, pieces[span], ((1,), (0,))
        )
        return unused

    lax.fori_loop(0, spans, intra, 0)

    gather_ends(ends_s, to_later, lambda far: place >= far)

    def before_copy(block):
        return remote(
            out.at[pl.ds((spans + block) * Q, Q), :], out.at[pl.ds(block * Q, Q), :],
            n_send.at[2 + block], n_recv.at[2 + block], "ctx", onward,
        )

    def outputs(span, unused):
        rows = span_rows(span)
        state = carry[...]
        whole = (starts[span] + state).astype(BF16)
        grown = over_columns(jnp.exp(cum_all[rows, :]), spread)
        out[span_rows(span + reach), :] = (
            y_intra[rows, :] + dot(c_all[rows, :], whole, ((1,), (1,))) * grown
        ).astype(BF16)
        for block in range(reach):

            @pl.when((span == spans - reach + block) & (place < ctx - 1))
            def _(block=block):
                before_copy(block).start()

        scaled = (g[rows, :].astype(F32) * grown).astype(BF16)
        grads[rows, pl.ds(0, N)] = db[rows, :].astype(BF16)
        grads[rows, pl.ds(N, N)] = (dc[rows, :] + dot(scaled, whole, ((1,), (0,)))).astype(BF16)
        carry[...] = over_rows(jnp.exp(cumt_all[span][:, Q - 1 : Q]), spread) * state
        return unused

    lax.fori_loop(0, spans, outputs, 0)
    shares = [
        remote(
            grads.at[token_rows(lax.rem(me + shift, groups)), :], parts.at[shift - 1],
            z_send.at[5, shift], z_recv.at[5, shift], "head", lax.rem(me + shift, groups),
        )
        for shift in range(1, groups)
    ]
    for copy in shares:
        copy.start()

    def mix(span, unused):
        own_rows = out[span_rows(span + reach), :].astype(F32)
        for far in range(1, reach + 1):
            own_rows = own_rows + picked(span, far) * out[span_rows(span + reach - far), :].astype(F32)
        mixed[span_rows(span), :] = own_rows.astype(BF16)
        return unused

    lax.fori_loop(reach, spans, mix, 0)

    @pl.when(place > 0)
    def _():
        for block in range(reach):
            before_copy(block).wait_recv()

    lax.fori_loop(0, reach, mix, 0)

    summed = grads[token_rows(me), :].astype(F32)
    for shift in range(1, groups):
        shares[shift - 1].wait_recv()
        summed = summed + parts[shift - 1].astype(F32)
    gb[...] = summed[:, :N]
    gc[...] = summed[:, N:]

    keep.wait()
    for copy in small + large + shares:
        copy.wait_send()
    for chunk in range(groups):

        @pl.when(me != chunk)
        def _(chunk=chunk):
            dx_copy(chunk).wait_send()
            remote(
                dx.at[pl.ds(0, tok_dev), :], gx.at[:, pl.ds(chunk * width, width)],
                z_send.at[4, chunk], z_recv.at[4, chunk], "head", chunk,
            ).wait_recv()

    @pl.when(place > 0)
    def _():
        for copy in later:
            copy.wait_send()

    @pl.when(place < ctx - 1)
    def _():
        for block in range(reach):
            before_copy(block).wait_send()

    for far in range(1, ctx):

        @pl.when(place >= far)
        def _(far=far):
            to_earlier[far - 1].wait_send()

        @pl.when(place + far < ctx)
        def _(far=far):
            to_later[far - 1].wait_send()


def body(channels, b_own, c_own, dt_own, a_log, skip_gain, mix_gain, offsets, cotangent):
    groups = lax.axis_size("head")
    ctx = lax.axis_size("ctx")
    tok_dev = channels.shape[0]
    tokens = tok_dev * groups
    spans = tokens // Q
    reach = spans // 2
    heads = a_log.shape[0]
    width = heads * P_SIZE
    in_scale = 1.0 / math.sqrt(N * tokens * ctx)
    pad = -(-heads // 16) * 16
    skip = jnp.repeat(skip_gain, P_SIZE)[None, :]
    gain = jnp.repeat(mix_gain.T, P_SIZE, axis=1)
    offs = jnp.pad(offsets, ((0, 0), (0, N - offsets.shape[1])))[:, None, :]
    held = pl.BlockSpec(memory_space=pl.ANY)
    here = pl.BlockSpec(memory_space=pltpu.VMEM)
    dma = pltpu.SemaphoreType.DMA
    args = (channels, b_own, c_own, dt_own, a_log[None, :], skip, gain, offs, cotangent)

    def kernel(*refs):
        mixer_kernel(groups, ctx, spans, reach, in_scale, *refs)

    return pl.pallas_call(
        kernel,
        out_shape=[
            jax.ShapeDtypeStruct((tokens, width), BF16),
            jax.ShapeDtypeStruct(channels.shape, BF16),
            jax.ShapeDtypeStruct((tok_dev, N), F32),
            jax.ShapeDtypeStruct((tok_dev, N), F32),
        ],
        in_specs=[held, held, held, held, here, here, here, held, held],
        out_specs=[here, held, here, here],
        scratch_shapes=[
            pltpu.VMEM(((spans + reach) * Q, width), BF16),
            pltpu.VMEM((spans + reach, 1, N), jnp.int32),
            pltpu.VMEM((tokens, N), BF16),
            pltpu.VMEM((tokens, N), BF16),
            pltpu.VMEM((tokens, dt_own.shape[1]), BF16),
            pltpu.VMEM((tokens, width), BF16),
            pltpu.VMEM((tokens, width), BF16),
            pltpu.VMEM((tokens, heads), F32),
            pltpu.VMEM((spans, heads, Q), F32),
            pltpu.VMEM((spans, width, N), BF16),
            pltpu.VMEM((width + pad, N), BF16),
            pltpu.VMEM((ctx - 1, width + pad, N), BF16),
            pltpu.VMEM((width + pad, N), BF16),
            pltpu.VMEM((ctx - 1, width + pad, N), BF16),
            pltpu.VMEM((spans, width, N), BF16),
            pltpu.VMEM((tokens, width), BF16),
            pltpu.VMEM((spans, width, N), F32),
            pltpu.VMEM((tokens, width), F32),
            pltpu.VMEM((tokens, N), F32),
            pltpu.VMEM((tokens, N), F32),
            pltpu.VMEM((tokens, 2 * N), BF16),
            pltpu.VMEM((groups - 1, tok_dev, 2 * N), BF16),
            pltpu.VMEM(((spans + reach) * Q, width), BF16),
            pltpu.VMEM((width, N), F32),
            pltpu.VMEM((heads, N), F32),
            dma((6, groups)),
            dma((6, groups)),
            dma((2, ctx)),
            dma((2, ctx)),
            dma((2 + reach,)),
            dma((2 + reach,)),
            dma((7,)),
        ],
        compiler_params=pltpu.CompilerParams(
            collective_id=0, has_side_effects=True, vmem_limit_bytes=VMEM_BYTES
        ),
    )(*args)


def solution(mesh):
    by_token = P(("ctx", "head"), None)
    return jax.shard_map(
        body,
        mesh=mesh,
        in_specs=(
            by_token, by_token, by_token, by_token, P("head"), P("head"), P("head", None),
            P("ctx", None), P("ctx", "head"),
        ),
        out_specs=(P("ctx", "head"), by_token, by_token, by_token),
        check_vma=False,
    )
```

profile of v0, /device:TPU:30, one launch (start us, length us, event | category | flops | bytes accessed | tf_op | source)
XLA Modules:
  0.0 114.9 jit_solution(6006615821017222471)
XLA Ops:
  0.6 0.8 copy.13
  1.4 0.6 broadcast_in_dim.15.refs_7_
  2.0 0.7 broadcast_in_dim.13
  2.7 0.7 broadcast_in_dim_reshape.3.refs_5_
  3.4 0.8 broadcast_in_dim.14
  4.1 0.7 reshape.11.refs_6_
  4.8 1.5 %copy.14.refs_3_ = bf16[192,64]{1,0:T(8,128)(2,1)} copy(bf16[192,64]{0,1:T(8,128)(2,1)} %param.12) | data formatting | bytes 49152 | tf_op args[3]
  6.3 103.3 %shard_map.120 = (bf16[768,1024]{1,0:T(8,128)(2,1)}, bf16[192,4096]{1,0:T(8,128)(2,1)}, f32[192,128]{1,0:T(8,128)}, f32[192,128]{1,0:T(8,128)}) custom-call(bf16[192,4096]{1,0:T(8,128)(2,1)} %refs_0_.1, bf16[192,128]{1,0:T(8,128)(2,1)} %refs_1_.1, bf16[192,128]{1,0:T(8,128)(2,1)} %refs_2_.1, bf16[192,64]{1,0:T(8,128)(2,1)} %copy.14.refs_3_, ...), custom_call_target="tpu_custom_call" | custom-call | tf_op jit(solution)/shard_map/pallas_call | solution.py:480
  109.7 0.0 copy-start
  109.7 2.8 %copy.19 = bf16[768,1024]{1,0:T(8,128)(2,1)} copy(bf16[768,1024]{1,0:T(8,128)(2,1)} %get-tuple-element.8) | data formatting | bytes 3145728
  112.5 0.0 copy-done
  112.5 0.0 copy-start.2
  112.5 0.0 copy-start.1
  112.5 1.1 copy.20
  113.6 0.0 copy-done.2
  113.6 0.6 copy.21
  114.3 0.0 copy-done.1
  114.3 0.6 copy.22
  (1 shorter events, 0.0 us)
Async XLA Ops:
  109.7 2.8 %copy-start = (bf16[192,4096]{1,0:T(8,128)(2,1)S(1)}, bf16[192,4096]{1,0:T(8,128)(2,1)}, u32[]{:S(2)}) copy-start(bf16[192,4096]{1,0:T(8,128)(2,1)} %get-tuple-element.9) | copy-start | bytes 4718596
  112.5 1.1 %copy-start.2 = (f32[192,128]{1,0:T(8,128)S(1)}, f32[192,128]{1,0:T(8,128)}, u32[]{:S(2)}) copy-start(f32[192,128]{1,0:T(8,128)} %get-tuple-element.10) | copy-start | bytes 294916
  112.5 1.8 %copy-start.1 = (f32[192,128]{1,0:T(8,128)S(1)}, f32[192,128]{1,0:T(8,128)}, u32[]{:S(2)}) copy-start(f32[192,128]{1,0:T(8,128)} %get-tuple-element.11) | copy-start | bytes 294916
where the time goes:
time: 115 us
  Pallas kernels  103 us (90%)
  local copies, waits for them, and re-layouts  10.9 us (9%)
    pallas_call x1, Pallas kernels, body(): pl.pallas_call(kernel, out_shape=[jax.ShapeDtypeStruct((tokens, width), B...  103 us
    unnamed x12, local copies, waits for them, and re-layouts  7.47 us

commit v1 on v0

--- a/solution.py
+++ b/solution.py
@@ -68,7 +68,7 @@
     groups, ctx, spans, reach, in_scale,
     chan_in, b_in, c_in, dt_in, a_log, skip, gain, offs, cot_in,
     mixed, gx, gb, gc,
-    cot, off, b_all, c_all, dt_all, chan, g, cum_all, cumt_all, full, pay_g, ends_g, pay_s, ends_s,
+    cot, off, b_all, c_all, dt_all, chan, g, cum_all, cumt_all, full, pay_g, other_g, both_g, ends_g, pay_s, other_s, both_s, ends_s,
     pieces, dx, starts, y_intra, db, dc, grads, parts, out, carry, running,
     z_send, z_recv, c_send, c_recv, n_send, n_recv, local,
 ):
@@ -181,14 +181,22 @@
         return total + cumt[:, Q - 1 : Q]
 
     total = lax.fori_loop(0, spans, add_up, jnp.zeros((heads, 1), F32))
-    high, low = halves(jnp.broadcast_to(total, (heads, N)))
-    lowest = (total - high.astype(F32) - low.astype(F32)).astype(BF16)
-    lane = iota((heads, N), 1)
-    packed = jnp.where(lane == 0, high, jnp.where(lane == 1, low, lowest))
     pad = pay_g.shape[0] - width
-    if pad > heads:
-        packed = jnp.concatenate([packed, jnp.zeros((pad - heads, N), BF16)], axis=0)
+
+    def log_rows(value):
+        value = jnp.broadcast_to(value, (heads, N))
+        high, low = halves(value)
+        lowest = (value - high.astype(F32) - low.astype(F32)).astype(BF16)
+        lane = iota((heads, N), 1)
+        rows = jnp.where(lane == 0, high, jnp.where(lane == 1, low, lowest))
+        if pad > heads:
+            rows = jnp.concatenate([rows, jnp.zeros((pad - heads, N), BF16)], axis=0)
+        return rows
+
+    packed = log_rows(total)
     pay_g[pl.ds(width, pad), :] = packed
+    core = lax.rem(place, 2)
+    sibling = place + 1 - 2 * core
     pay_s[pl.ds(width, pad), :] = packed
 
     @pl.when(place < ctx - 1)
@@ -226,18 +234,39 @@
         return [
             remote(
                 source, ends.at[far - 1], c_send.at[kind, far], c_recv.at[kind, far], "ctx",
-                lax.rem(place + ctx + sign * far, ctx),
+                lax.rem(place + ctx + 2 * sign * far, ctx),
             )
-            for far in range(1, ctx)
+            for far in range(1, ctx // 2)
         ]
 
-    to_earlier = scan_copies(0, pay_g, ends_g, -1)
-    to_later = scan_copies(1, pay_s, ends_s, 1)
-
-    def gather_ends(ends, copies, present):
-        carry[...] = jnp.zeros_like(carry)
-        running[...] = jnp.zeros_like(running)
-        for far in range(1, ctx):
+    to_earlier = scan_copies(0, both_g, ends_g, -1)
+    to_later = scan_copies(1, both_s, ends_s, 1)
+
+    def log_column(ref):
+        logs = ref[pl.ds(width, pad), :].astype(F32)[:heads]
+        return logs[:, 0:1] + logs[:, 1:2] + logs[:, 2:3]
+
+    def pair_up(kind, pay, other, both, nearer):
+        copy = remote(pay, other, c_send.at[kind, 0], c_recv.at[kind, 0], "ctx", sibling)
+        copy.start()
+        near = nearer.astype(F32)
+        own_log = jnp.broadcast_to(total, (heads, N))[:, :1]
+        copy.wait_recv()
+        other_log = log_column(other)
+        joint = over_rows(jnp.exp((1.0 - near) * other_log), spread) * pay[
+            pl.ds(0, width), :
+        ].astype(F32) + over_rows(jnp.exp(near * own_log), spread) * other[
+            pl.ds(0, width), :
+        ].astype(F32)
+        both[pl.ds(0, width), :] = joint.astype(BF16)
+        both[pl.ds(width, pad), :] = log_rows(own_log + other_log)
+        return copy
+
+    def gather_ends(other, nearer, ends, copies, present):
+        near = nearer.astype(F32)
+        carry[...] = near * other[pl.ds(0, width), :].astype(F32)
+        running[...] = jnp.broadcast_to(near * log_column(other), running.shape)
+        for far in range(1, ctx // 2):
 
             @pl.when(present(far))
             def _(far=far):
@@ -249,9 +278,10 @@
                 logs = ends[far - 1, pl.ds(width, pad), :].astype(F32)[:heads]
                 running[...] = sums + (logs[:, 0:1] + logs[:, 1:2] + logs[:, 2:3])
 
-    for far in range(1, ctx):
-
-        @pl.when(place >= far)
+    pair_g = pair_up(0, pay_g, other_g, both_g, core == 0)
+    for far in range(1, ctx // 2):
+
+        @pl.when(place >= 2 * far)
         def _(far=far):
             to_earlier[far - 1].start()
 
@@ -277,13 +307,14 @@
 
     lax.fori_loop(0, spans, add_pieces, 0)
     pay_s[pl.ds(0, width), :] = carry[...].astype(BF16)
-    for far in range(1, ctx):
-
-        @pl.when(place + far < ctx)
+    pair_s = pair_up(1, pay_s, other_s, both_s, core == 1)
+    for far in range(1, ctx // 2):
+
+        @pl.when(place // 2 + far < ctx // 2)
         def _(far=far):
             to_later[far - 1].start()
 
-    gather_ends(ends_g, to_earlier, lambda far: place + far < ctx)
+    gather_ends(other_g, core == 0, ends_g, to_earlier, lambda far: place // 2 + far < ctx // 2)
 
     def dx_copy(chunk):
         return remote(
@@ -359,7 +390,7 @@
 
     lax.fori_loop(0, spans, intra, 0)
 
-    gather_ends(ends_s, to_later, lambda far: place >= far)
+    gather_ends(other_s, core == 1, ends_s, to_later, lambda far: place >= 2 * far)
 
     def before_copy(block):
         return remote(
@@ -422,6 +453,8 @@
     gc[...] = summed[:, N:]
 
     keep.wait()
+    pair_g.wait_send()
+    pair_s.wait_send()
     for copy in small + large + shares:
         copy.wait_send()
     for chunk in range(groups):
@@ -444,13 +477,13 @@
         for block in range(reach):
             before_copy(block).wait_send()
 
-    for far in range(1, ctx):
-
-        @pl.when(place >= far)
+    for far in range(1, ctx // 2):
+
+        @pl.when(place >= 2 * far)
         def _(far=far):
             to_earlier[far - 1].wait_send()
 
-        @pl.when(place + far < ctx)
+        @pl.when(place // 2 + far < ctx // 2)
         def _(far=far):
             to_later[far - 1].wait_send()
 
@@ -499,9 +532,13 @@
             pltpu.VMEM((spans, heads, Q), F32),
             pltpu.VMEM((spans, width, N), BF16),
             pltpu.VMEM((width + pad, N), BF16),
-            pltpu.VMEM((ctx - 1, width + pad, N), BF16),
             pltpu.VMEM((width + pad, N), BF16),
-            pltpu.VMEM((ctx - 1, width + pad, N), BF16),
+            pltpu.VMEM((width + pad, N), BF16),
+            pltpu.VMEM((ctx // 2 - 1, width + pad, N), BF16),
+            pltpu.VMEM((width + pad, N), BF16),
+            pltpu.VMEM((width + pad, N), BF16),
+            pltpu.VMEM((width + pad, N), BF16),
+            pltpu.VMEM((ctx // 2 - 1, width + pad, N), BF16),
             pltpu.VMEM((spans, width, N), BF16),
             pltpu.VMEM((tokens, width), BF16),
             pltpu.VMEM((spans, width, N), F32),

time: 115 us -> 115 us (level)
  the two profiles are of different devices: /device:TPU:30 before, /device:TPU:8 now
where the time goes in v1:
time: 115 us; the launch traced here: 114 us
  Pallas kernels  102 us (89%)
  local copies, waits for them, and re-layouts  10.9 us (9%)
    pallas_call x1, Pallas kernels, body(): pl.pallas_call(kernel, out_shape=[jax.ShapeDtypeStruct((tokens, width), B...  102 us
    unnamed x12, local copies, waits for them, and re-layouts  7.47 us

profile of v1, /device:TPU:8, one launch (start us, length us, event | category | flops | bytes accessed | tf_op | source)
XLA Modules:
  0.0 113.8 jit_solution(7133440455238599875)
XLA Ops:
  0.6 0.8 copy.13
  1.4 0.6 broadcast_in_dim.15.refs_7_
  2.0 0.7 broadcast_in_dim.13
  2.7 0.7 broadcast_in_dim_reshape.3.refs_5_
  3.4 0.8 broadcast_in_dim.14
  4.1 0.7 reshape.11.refs_6_
  4.8 1.5 %copy.14.refs_3_ = bf16[192,64]{1,0:T(8,128)(2,1)} copy(bf16[192,64]{0,1:T(8,128)(2,1)} %param.12) | data formatting | bytes 49152 | tf_op args[3]
  6.3 102.2 %shard_map.120 = (bf16[768,1024]{1,0:T(8,128)(2,1)}, bf16[192,4096]{1,0:T(8,128)(2,1)}, f32[192,128]{1,0:T(8,128)}, f32[192,128]{1,0:T(8,128)}) custom-call(bf16[192,4096]{1,0:T(8,128)(2,1)} %refs_0_.1, bf16[192,128]{1,0:T(8,128)(2,1)} %refs_1_.1, bf16[192,128]{1,0:T(8,128)(2,1)} %refs_2_.1, bf16[192,64]{1,0:T(8,128)(2,1)} %copy.14.refs_3_, ...), custom_call_target="tpu_custom_call" | custom-call | tf_op jit(solution)/shard_map/pallas_call | solution.py:513
  108.5 0.0 copy-start
  108.5 2.8 %copy.19 = bf16[768,1024]{1,0:T(8,128)(2,1)} copy(bf16[768,1024]{1,0:T(8,128)(2,1)} %get-tuple-element.8) | data formatting | bytes 3145728
  111.3 0.0 copy-done
  111.3 0.0 copy-start.2
  111.3 0.0 copy-start.1
  111.3 1.1 %copy.20 = bf16[192,4096]{1,0:T(8,128)(2,1)} copy(bf16[192,4096]{1,0:T(8,128)(2,1)S(1)} %copy-done) | data formatting | bytes 3145728
  112.5 0.0 copy-done.2
  112.5 0.6 copy.21
  113.1 0.0 copy-done.1
  113.1 0.6 copy.22
  (1 shorter events, 0.0 us)
Async XLA Ops:
  108.5 2.8 %copy-start = (bf16[192,4096]{1,0:T(8,128)(2,1)S(1)}, bf16[192,4096]{1,0:T(8,128)(2,1)}, u32[]{:S(2)}) copy-start(bf16[192,4096]{1,0:T(8,128)(2,1)} %get-tuple-element.9) | copy-start | bytes 4718596
  111.3 1.1 %copy-start.2 = (f32[192,128]{1,0:T(8,128)S(1)}, f32[192,128]{1,0:T(8,128)}, u32[]{:S(2)}) copy-start(f32[192,128]{1,0:T(8,128)} %get-tuple-element.10) | copy-start | bytes 294916
  111.3 1.8 %copy-start.1 = (f32[192,128]{1,0:T(8,128)S(1)}, f32[192,128]{1,0:T(8,128)}, u32[]{:S(2)}) copy-start(f32[192,128]{1,0:T(8,128)} %get-tuple-element.11) | copy-start | bytes 294916
